TPU v7x, 512 devices: a whole 4x8x8 slice. The times are simulated.
512 devices in a mesh: row: 32 (over z, y_hi), col: 16 (over y_lo, x, core).
Axes of the slice: x: 4, y: 8 (y_hi: 4, y_lo: 2; y = y_hi * 2 + y_lo), z: 8, core: 2. Of those that a mesh axis runs over, the one named last changes fastest.
Arguments:
- orbitals: bfloat16 [20480, 384], P(('row', 'col')), may hold values from -6 to 6
- coulomb: float32 [20480, 20480], P('row', 'col'), may hold values from -0.001953125 to 0.001953125
- interp: bfloat16 [16384, 20480], P('row', 'col'), may hold values from -0.0390625 to 0.0390625
Outputs:
- exchanged: bfloat16 [16384, 384], P(('row', 'col'))
All inputs are finite; a program needn't handle non-finite values.
Results may differ from a plain program's by a relative error of at most 0.018.
Values may be sent and summed in bfloat16 or wider, within the bound.
A program may use at most 64 MiB of HBM per device.

v0:
```python
import jax
import jax.numpy as jnp
from jax import lax
from jax.sharding import PartitionSpec as P


def broadcast(value, axis, source):
    kept = jnp.where(lax.axis_index(axis) == source, value, 0).astype(value.dtype)
    return lax.psum(kept, axis)


def local(orbitals, coulomb, interp):
    near = lax.all_gather(orbitals, "col", axis=0, tiled=True)
    factor = lax.axis_size("row") // lax.axis_size("col")
    column = lax.axis_index("col")
    pieces = []
    for offset in range(factor):
        pieces.append(broadcast(near, "row", column * factor + offset))
    far = jnp.concatenate(pieces, 0)
    density = lax.dot_general(
        near, far, (((1,), (1,)), ((), ())), preferred_element_type=jnp.float32
    )
    weighted = (coulomb * density).astype(jnp.bfloat16)
    partial_sum = lax.dot_general(
        weighted, near, (((0,), (0,)), ((), ())), preferred_element_type=jnp.float32
    )
    summed = lax.psum(partial_sum, "row")
    contracted = summed.astype(jnp.bfloat16)
    terms = jnp.dot(interp, contracted, preferred_element_type=jnp.float32)
    return lax.psum_scatter(terms.astype(jnp.bfloat16), "col", scatter_dimension=0, tiled=True)


def solution(mesh):
    in_specs = (P(("row", "col"), None), P("row", "col"), P("row", "col"))
    out_specs = P(("row", "col"), None)
    return jax.shard_map(local, mesh=mesh, in_specs=in_specs, out_specs=out_specs, check_vma=False)
```

profile of v0, /device:TPU:16, one launch (start us, length us, event | category | flops | bytes accessed | tf_op | source)
XLA Modules:
  0.0 611.8 jit_solution(2543077804153859087)
XLA Ops:
  6.5 0.0 copy-start
  6.5 0.0 all-reduce.4.cloned.1.call-start
  6.5 21.4 %all_gather.3 = bf16[640,384]{1,0:T(8,128)(2,1)S(1)} all-gather(bf16[40,384]{1,0:T(8,128)(2,1)} %param.3), channel_id=1, replica_groups=mesh['row'=32,'col'=16] {'col'}, dimensions={0}, use_global_device_ids=true | all-gather | bytes 522240 | tf_op jit(solution)/shard_map/all_gather | solution.py:13
  27.9 0.0 copy-start.1
  27.9 0.8 copy-done.1
  28.7 1.0 broadcast_select_fusion.1
  29.7 0.0 all-reduce.4.cloned.1.call-update
  29.8 0.0 reduce-scatter.4.cloned.1.call-start
  29.8 318.4 %all-reduce.4.cloned.1.call-done = (bf16[640,384]{1,0:T(8,128)(2,1)}, bf16[640,384]{1,0:T(8,128)(2,1)}) async-done(((bf16[640,384]{1,0:T(8,128)(2,1)}, bf16[640,384]{1,0:T(8,128)(2,1)}), (bf16[640,384]{1,0:T(8,128)(2,1)}, bf16[640,384]{1,0:T(8,128)(2,1)})) %all-reduce.4.cloned.1.call-update) | async-done | bytes 983056 | tf_op jit(solution)/shard_map/psum | solution.py:9
  348.3 4.4 fusion.2
  352.7 185.9 %all-reduce.5 = bf16[1280,384]{1,0:T(8,128)(2,1)} all-reduce(f32[1280,384]{1,0:T(8,128)S(1)} %fusion.2), channel_id=1, replica_groups=mesh['row'=32,'col'=16] {'row'}, use_global_device_ids=true, to_apply=%region_2.3 | all-reduce | flops 491520 | bytes 2949120 | tf_op jit(solution)/shard_map/psum | solution.py:27
  538.6 0.0 copy-done
  538.6 1.9 fusion.3
  540.5 0.9 copy.6
  541.5 0.0 reduce-scatter.4.cloned.1.call-update
  541.5 63.5 %reduce-scatter.4.cloned.1.call-done = bf16[32,384]{1,0:T(8,128)(2,1)} async-done(((bf16[512,384]{1,0:T(8,128)(2,1)}), bf16[32,384]{1,0:T(8,128)(2,1)}) %reduce-scatter.4.cloned.1.call-update) | async-done | bytes 24592 | tf_op jit(solution)/shard_map/reduce_scatter | solution.py:30
Async XLA Ops:
  6.5 532.1 %copy-start = (bf16[512,1280]{1,0:T(8,128)(2,1)S(1)}, bf16[512,1280]{1,0:T(8,128)(2,1)}, u32[]{:S(2)}) copy-start(bf16[512,1280]{1,0:T(8,128)(2,1)} %param.5) | copy-start | bytes 3932164
  6.5 341.7 %all-reduce.4.cloned.1.call-start = ((), (), s32[]{:S(2)}) async-start(), calls=%async_computation.2 | async-start | bytes 1966080 | tf_op jit(solution)/shard_map/psum | solution.py:9
  27.9 0.8 copy-start.1
  29.8 575.2 %reduce-scatter.4.cloned.1.call-start = ((), (), s32[]{:S(2)}) async-start(), calls=%async_computation.1 | async-start | bytes 417792 | tf_op jit(solution)/shard_map/reduce_scatter | solution.py:30
Sparse Core Ops, SparseCore 0:
  29.9 318.3 all-reduce.3
  541.6 63.3 reduce-scatter.3
where the time goes:
time: 612 us
  waiting for transfers between devices  382 us (62%)
  blocking collectives  207 us (34%)
  between operations  13.4 us (2%)
  matrix products  6.34 us (1%)
    psum x1, waiting for transfers between devices, broadcast(): return lax.psum(kept, axis)  318 us
    psum x1, blocking collectives, local(): summed = lax.psum(partial_sum, 'row')  186 us
    reduce_scatter x1, waiting for transfers between devices, local(): lax.psum_scatter(terms.astype(jnp.bfloat16), 'col', scatter_dimension=0,...  63.5 us
    all_gather x1, blocking collectives, local(): near = lax.all_gather(orbitals, 'col', axis=0, tiled=True)  21.4 us
  transfers between devices with their start and end apart: 2, of which 2 were waited for; matrix products, arithmetic and copies ran while one was open for 0% of the time, Pallas kernels for 0%

commit v1 on v0

--- a/solution.py
+++ b/solution.py
@@ -6,7 +6,7 @@
 
 def broadcast(value, axis, source):
     kept = jnp.where(lax.axis_index(axis) == source, value, 0).astype(value.dtype)
-    return lax.psum(kept, axis)
+    return jnp.sum(lax.all_gather(kept, axis), axis=0)
 
 
 def local(orbitals, coulomb, interp):

time: 612 us -> 718 us (1.17)
  waiting for transfers between devices: 382 us -> 472 us
  other arithmetic: 1.03 us -> 19.5 us
    all_gather x0 -> x2, waiting for transfers between devices: none -> 404 us  [broadcast(): return jnp.sum(lax.all_gather(kept, axis), axis=0)]
    psum x1 -> x0, waiting for transfers between devices: 318 us -> none  [broadcast(): return lax.psum(kept, axis)]
    reduce_sum x0 -> x2, other arithmetic: none -> 18.4 us  [broadcast(): return jnp.sum(lax.all_gather(kept, axis), axis=0)]
  transfers between devices with their start and end apart: 2 -> 3, of which waited for: 2 -> 3; matrix products, arithmetic and copies ran while one was open for 0% -> 1% of each run, Pallas kernels for 0% -> 0%
where the time goes in v1:
time: 718 us
  waiting for transfers between devices  472 us (66%)
  blocking collectives  205 us (29%)
  other arithmetic  19.5 us (3%)
  between operations  13.1 us (2%)
    all_gather x2, waiting for transfers between devices, broadcast(): return jnp.sum(lax.all_gather(kept, axis), axis=0)  404 us
    psum x1, blocking collectives, local(): summed = lax.psum(partial_sum, 'row')  184 us
    reduce_scatter x1, waiting for transfers between devices, local(): lax.psum_scatter(terms.astype(jnp.bfloat16), 'col', scatter_dimension=0,...  66.8 us
    all_gather x1, blocking collectives, local(): near = lax.all_gather(orbitals, 'col', axis=0, tiled=True)  21.4 us
    reduce_sum x2, other arithmetic, broadcast(): return jnp.sum(lax.all_gather(kept, axis), axis=0)  18.4 us
  transfers between devices with their start and end apart: 3, of which 3 were waited for; matrix products, arithmetic and copies ran while one was open for 1% of the time, Pallas kernels for 0%

profile of v1, /device:TPU:16, one launch (start us, length us, event | category | flops | bytes accessed | tf_op | source)
XLA Modules:
  0.0 718.0 jit_solution(186762104237527439)
XLA Ops:
  6.5 0.0 copy-start
  6.5 0.0 all-gather.5.cloned.1.call-start
  6.5 21.4 %all_gather.15 = bf16[640,384]{1,0:T(8,128)(2,1)S(1)} all-gather(bf16[40,384]{1,0:T(8,128)(2,1)} %param.3), channel_id=1, replica_groups=mesh['row'=32,'col'=16] {'col'}, dimensions={0}, use_global_device_ids=true | all-gather | bytes 522240 | tf_op jit(solution)/shard_map/all_gather | solution.py:13
  27.9 0.0 copy-start.1
  27.9 0.8 copy-done.1
  28.7 1.1 broadcast_select_fusion.1
  29.8 0.0 all-gather.5.cloned.1.call-update
  29.8 0.0 all-gather.7.cloned.1.call-start
  29.9 0.7 all-gather.7.cloned.1.call-update
  30.6 0.0 reduce-scatter.4.cloned.1.call-start
  30.6 207.2 %all-gather.5.cloned.1.call-done = bf16[20480,384]{1,0:T(8,128)(2,1)} async-done(((bf16[640,384]{1,0:T(8,128)(2,1)}), bf16[20480,384]{1,0:T(8,128)(2,1)}) %all-gather.5.cloned.1.call-update) | async-done | bytes 15728656 | tf_op jit(solution)/shard_map/all_gather | solution.py:9
  237.9 9.2 %reduce_sum.24 = bf16[640,384]{1,0:T(8,128)(2,1)} reduce(bf16[32,640,384]{2,1,0:T(8,128)(2,1)} %bitcast.17, bf16[]{:T(256)} %constant.17.clone.1), dimensions={0}, to_apply=%region_0.1 | reduce | flops 7618560 | bytes 16220162 | tf_op jit(solution)/shard_map/reduce_sum | solution.py:9
  247.1 196.9 %all-gather.7.cloned.1.call-done = bf16[20480,384]{1,0:T(8,128)(2,1)} async-done(((bf16[640,384]{1,0:T(8,128)(2,1)}), bf16[20480,384]{1,0:T(8,128)(2,1)}) %all-gather.7.cloned.1.call-update) | async-done | bytes 15728656 | tf_op jit(solution)/shard_map/all_gather | solution.py:9
  444.0 9.2 %reduce_sum.25 = bf16[640,384]{1,0:T(8,128)(2,1)} reduce(bf16[32,640,384]{2,1,0:T(8,128)(2,1)} %bitcast.18, bf16[]{:T(256)} %constant.17.clone.1), dimensions={0}, to_apply=%region_1.2 | reduce | flops 7618560 | bytes 16220162 | tf_op jit(solution)/shard_map/reduce_sum | solution.py:9
  453.3 4.4 fusion.2
  457.7 184.1 %all-reduce.1 = bf16[1280,384]{1,0:T(8,128)(2,1)} all-reduce(f32[1280,384]{1,0:T(8,128)S(1)} %fusion.2), channel_id=1, replica_groups=mesh['row'=32,'col'=16] {'row'}, use_global_device_ids=true, to_apply=%region_2.3 | all-reduce | flops 491520 | bytes 2949120 | tf_op jit(solution)/shard_map/psum | solution.py:27
  641.8 0.0 copy-done
  641.8 1.9 fusion.3
  643.7 0.9 copy.6
  644.6 0.0 reduce-scatter.4.cloned.1.call-update
  644.6 66.8 %reduce-scatter.4.cloned.1.call-done = bf16[32,384]{1,0:T(8,128)(2,1)} async-done(((bf16[512,384]{1,0:T(8,128)(2,1)}), bf16[32,384]{1,0:T(8,128)(2,1)}) %reduce-scatter.4.cloned.1.call-update) | async-done | bytes 24592 | tf_op jit(solution)/shard_map/reduce_scatter | solution.py:30
Async XLA Ops:
  6.5 635.2 %copy-start = (bf16[512,1280]{1,0:T(8,128)(2,1)S(1)}, bf16[512,1280]{1,0:T(8,128)(2,1)}, u32[]{:S(2)}) copy-start(bf16[512,1280]{1,0:T(8,128)(2,1)} %param.5) | copy-start | bytes 3932164
  6.5 231.3 %all-gather.5.cloned.1.call-start = ((), (), s32[]{:S(2)}) async-start(), calls=%async_computation.1 | async-start | bytes 16220160 | tf_op jit(solution)/shard_map/all_gather | solution.py:9
  27.9 0.8 copy-start.1
  29.8 414.2 %all-gather.7.cloned.1.call-start = ((), (), s32[]{:S(2)}) async-start(), calls=%async_computation.2 | async-start | bytes 16220160 | tf_op jit(solution)/shard_map/all_gather | solution.py:9
  30.6 680.8 %reduce-scatter.4.cloned.1.call-start = ((), (), s32[]{:S(2)}) async-start(), calls=%async_computation.3 | async-start | bytes 417792 | tf_op jit(solution)/shard_map/reduce_scatter | solution.py:30
Sparse Core Ops, SparseCore 0:
  30.0 207.8 all-gather.4
  241.0 202.9 all-gather.6
  644.8 66.6 reduce-scatter.3
